TPU v7x, 256 devices: a whole 4x4x8 slice. The times are simulated.
256 devices in a mesh: rep: 16 (over y, z_hi, core), shard: 16 (over z_lo, x).
Axes of the slice: x: 4, y: 4, z: 8 (z_hi: 2, z_lo: 4; z = z_hi * 4 + z_lo), core: 2. Of those that a mesh axis runs over, the one named last changes fastest.
Arguments:
- theta_outer: bfloat16 [16, 4096, 1792], P('rep', 'shard'), may hold values from -6 to 6
- theta_local: bfloat16 [16, 4096, 1792], P('rep', 'shard'), may hold values from -6 to 6
- momentum: float32 [16, 4096, 1792], P('rep', 'shard'), may hold values from -6 to 6
- gate_pre: bfloat16 [16, 4096, 1792], P('rep', 'shard'), may hold values from -8 to 8
- up_pre: bfloat16 [16, 4096, 1792], P('rep', 'shard'), may hold values from -6 to 6
- cotangent: bfloat16 [16, 4096, 4096], P('rep', 'shard'), may hold values from -6 to 6
- partner: int32 [16, 16], P('shard'), may hold values from 0 to 15, as said below
- chosen: int32 [16, 14], P('shard'), may hold values from 0 to 27, as said below
Outputs:
- momentum_new: float32 [16, 4096, 1792], P('rep', 'shard')
- grad_weight: bfloat16 [16, 4096, 1792], P('rep', 'shard')
- grad_gate: bfloat16 [16, 4096, 1792], P('rep', 'shard')
- grad_up: bfloat16 [16, 4096, 1792], P('rep', 'shard')
Inputs may be any that keep to these rules, and one draw needn't show every extreme that they name: For each shard s, partner[s, r] equals r XOR m_s for one number m_s of 1 to 15 that is common to all replicas of that shard, so partner[s, partner[s, r]] = r. `chosen`: each row holds 14 distinct tile indices.
All inputs are finite; a program needn't handle non-finite values.
Results may differ from a plain program's by a relative error of at most 0.023.
Values may be sent and summed in bfloat16 or wider, within the bound.
No kernel may reach another device: no remote copies, remote signals or barrier semaphores. Data moves between devices by JAX's collectives and lax.ppermute only.
A program may use at most 128 MiB of HBM per device.

v0:
```python
import functools

import jax
import jax.numpy as jnp
from jax import lax
from jax.experimental import pallas as pl
from jax.experimental.pallas import tpu as pltpu
from jax.sharding import Mesh
from jax.sharding import PartitionSpec as P

TILE = 128
SIDE = 4
OUTER_RATE = 0.7
OUTER_MU = 0.9
ALL_VMEM = 60 * 2**20
VMEM = pl.BlockSpec(memory_space=pltpu.VMEM)
SMEM = pl.BlockSpec(memory_space=pltpu.SMEM)


def step_kernel(chosen_ref, outer_ref, local_ref, moment_ref, moved_ref, moment_out, theta_out, place):
    across = outer_ref.shape[1] // TILE
    first = (pl.program_id(0) * pl.num_programs(1) + pl.program_id(1)) * across

    @pl.when(first == 0)
    def _():
        for t in range(place.shape[0]):
            place[t] = -1
        for i in range(moved_ref.shape[0]):
            place[chosen_ref[0, i]] = i

    for col in range(across):
        at = (slice(None), slice(col * TILE, (col + 1) * TILE))
        found = place[first + col]
        outer = outer_ref[at].astype(jnp.float32)
        delta = (outer - local_ref[at].astype(jnp.float32)).astype(jnp.bfloat16).astype(jnp.float32)
        other = moved_ref[jnp.maximum(found, 0)].astype(jnp.float32)
        mixed = jnp.where(found >= 0, 0.5 * (delta + other), delta)
        moment = OUTER_MU * moment_ref[at] + mixed
        moment_out[at] = moment
        theta_out[at] = (outer - OUTER_RATE * (mixed + OUTER_MU * moment)).astype(jnp.bfloat16)


def outer_step(chosen, outer, local_rows, moment, moved):
    rows, width = outer.shape
    block = pl.BlockSpec((TILE, width // 2), lambda i, j: (i, j))
    tiles = pl.BlockSpec(moved.shape, lambda i, j: (0, 0, 0))
    return pl.pallas_call(
        step_kernel,
        grid=(rows // TILE, 2),
        out_shape=[
            jax.ShapeDtypeStruct((rows, width), jnp.float32),
            jax.ShapeDtypeStruct((rows, width), jnp.bfloat16),
        ],
        in_specs=[SMEM, block, block, block, tiles],
        out_specs=[block, block],
        scratch_shapes=[pltpu.SMEM((rows // TILE * (width // TILE),), jnp.int32)],
        compiler_params=pltpu.CompilerParams(vmem_limit_bytes=ALL_VMEM),
        cost_estimate=pl.CostEstimate(flops=8 * rows * width, bytes_accessed=14 * rows * width, transcendentals=0),
        name="outer_step",
    )(chosen, outer, local_rows, moment, moved)


def prepare_kernel(
    where_ref, chosen_ref, outer_ref, local_ref, gate_ref, up_ref, cot_ref, picked_out, hid_out, cot_out, go_up, go_down
):
    width = gate_ref.shape[2]
    across = cot_out.shape[2]
    piece = across // SIDE
    far = width + across
    gate = gate_ref[...].astype(jnp.float32)
    hidden = (gate * jax.nn.sigmoid(gate) * up_ref[...].astype(jnp.float32)).astype(jnp.bfloat16)
    hid_out[...] = hidden
    go_up[:, :width] = hidden[0]
    go_up[:, far : far + width] = hidden[1]
    go_down[:, :width] = hidden[1]
    go_down[:, far : far + width] = hidden[0]
    for k in range(SIDE):
        group = jnp.bitwise_xor(where_ref[0], k) * SIDE
        columns = []
        for by in range(SIDE):
            at = pl.multiple_of((group + (where_ref[1] + by) % SIDE) * piece, piece)
            columns.append(cot_ref[:, :, pl.ds(at, piece)])
        near, second = far + width + k * piece, far + width + across + k * piece
        cot_out[:, :, k * piece : (k + 1) * piece] = columns[0]
        go_up[:, near : near + piece] = columns[1][0]
        go_up[:, second : second + piece] = columns[1][1]
        go_up[:, width + k * piece : width + (k + 1) * piece] = columns[2][0]
        go_down[:, width + k * piece : width + (k + 1) * piece] = columns[2][1]
        go_down[:, near : near + piece] = columns[3][0]
        go_down[:, second : second + piece] = columns[3][1]

    tiles = width // TILE
    for i in range(picked_out.shape[0]):
        tile = chosen_ref[0, i]
        at = (tile // tiles, slice(None), pl.ds(pl.multiple_of(tile % tiles * TILE, TILE), TILE))
        delta = outer_ref[at].astype(jnp.float32) - local_ref[at].astype(jnp.float32)
        picked_out[i] = delta.astype(jnp.bfloat16)


def prepare(where, chosen, *arrays):
    rows, width = arrays[0].shape
    depth = arrays[-1].shape[1]
    half, across = rows // 2, depth // SIDE
    assert half == TILE
    step = half // 4
    halves = lambda n: pl.BlockSpec((2, step, n), lambda i: (0, i, 0))
    go = pl.BlockSpec((step, 2 * width + 3 * across), lambda i: (i, 0))
    shapes = [(chosen.shape[1], TILE, TILE), (2, half, width), (2, half, across)] + [(half, 2 * width + 3 * across)] * 2
    picked, hidden, own, go_up, go_down = pl.pallas_call(
        prepare_kernel,
        grid=(half // step,),
        out_shape=[jax.ShapeDtypeStruct(shape, jnp.bfloat16) for shape in shapes],
        in_specs=[SMEM, SMEM] + [halves(value.shape[1]) for value in arrays],
        out_specs=[
            pl.BlockSpec((chosen.shape[1], step, TILE), lambda i: (0, i, 0)), halves(width), halves(across), go, go,
        ],
        compiler_params=pltpu.CompilerParams(vmem_limit_bytes=ALL_VMEM),
        cost_estimate=pl.CostEstimate(flops=4 * rows * width, bytes_accessed=11 * 2**20, transcendentals=rows * width),
        name="prepare",
    )(where, chosen, *[value.reshape(2, half, value.shape[1]) for value in arrays])
    return picked, hidden.reshape(rows, width), own.reshape(rows, across), go_up, go_down


def gather_kernel(hidden, own, go_up, go_down, cot_out, hid_out):
    rows, width = hidden.shape
    half, across = rows // 2, own.shape[1]
    near = width + across
    first, second = slice(near + width, near + width + across), slice(near + width + across, near + width + 2 * across)
    far, other = slice(0, width), slice(near, near + width)
    cot_out[:rows] = own[...]
    hid_out[:rows] = hidden[...]
    for n, (ref, tokens, features) in enumerate(
        ((go_down, other, first), (go_down, far, second), (go_up, far, first), (go_up, other, second))
    ):
        to = slice(rows + n * half, rows + (n + 1) * half)
        cot_out[to] = ref[:, features]
        hid_out[to] = ref[:, tokens]


def gather_near(hidden, own, go_up, go_down):
    rows, width = hidden.shape
    sizes = [((SIDE - 1) * rows, own.shape[1]), ((SIDE - 1) * rows, width)]
    return pl.pallas_call(
        gather_kernel,
        out_shape=[jax.ShapeDtypeStruct(size, jnp.bfloat16) for size in sizes],
        in_specs=[VMEM] * 4,
        out_specs=[VMEM] * 2,
        compiler_params=pltpu.CompilerParams(vmem_limit_bytes=20 * 2**20),
        cost_estimate=pl.CostEstimate(flops=2**20, bytes_accessed=2**20, transcendentals=0),
        name="gather_near",
    )(hidden, own, go_up, go_down)


def weight_kernel(scale, cot, hid, last_up, last_down, cot_out, third_out, second_out, first_out, own_out, hid_far):
    step = pl.program_id(0)
    width = hid.shape[1]
    half, across = last_up.shape[0], cot.shape[1]
    piece = across // SIDE

    @pl.when(step == 0)
    def _():
        for ref, to in ((last_up, slice(0, half)), (last_down, slice(half, 2 * half))):
            cot_out[to] = ref[:, width:]
            hid_far[to] = ref[:, :width]

    for n, (which, out_ref) in enumerate(((3, third_out), (2, second_out), (1, first_out), (0, own_out))):

        @pl.when(step == n)
        def _(which=which, out_ref=out_ref):
            at = slice(which * piece, (which + 1) * piece)
            turned = (((0,), (0,)), ((), ()))
            part = lax.dot_general(cot[:, at], hid[...], turned, preferred_element_type=jnp.float32)
            part = part + lax.dot_general(cot_out[:, at], hid_far[...], turned, preferred_element_type=jnp.float32)
            out_ref[...] = (scale * part).astype(jnp.bfloat16)


def weight_parts(scale, cot, hid, *moved):
    width, across = hid.shape[1], cot.shape[1]
    rows = cot.shape[0] // (SIDE - 1)
    sizes = [(rows, across)] + [(across // SIDE, width)] * SIDE
    whole = lambda shape: pl.BlockSpec(shape, lambda i: (0, 0))
    return pl.pallas_call(
        functools.partial(weight_kernel, scale),
        grid=(SIDE,),
        out_shape=[jax.ShapeDtypeStruct(size, jnp.bfloat16) for size in sizes],
        in_specs=[whole(value.shape) for value in (cot, hid, *moved)],
        out_specs=[whole(size) for size in sizes],
        scratch_shapes=[pltpu.VMEM((rows, width), jnp.bfloat16)],
        compiler_params=pltpu.CompilerParams(vmem_limit_bytes=40 * 2**20),
        cost_estimate=pl.CostEstimate(flops=2**20, bytes_accessed=2**20, transcendentals=0),
        name="weight_parts",
    )(cot, hid, *moved)


def is_inner(z):
    return (z > 0) & (z < SIDE - 1)


def near_sum(z, cot_ref, own, beside, mid_inner, mid_outer):
    piece = own.shape[0]
    mid = jnp.where(is_inner(z), mid_inner[...], mid_outer[...])
    total = 0.0
    for k, block in enumerate((own[...], beside[...], mid)):
        total = total + jnp.dot(cot_ref[:, k * piece : (k + 1) * piece], block, preferred_element_type=jnp.float32)
    return total


def with_last(z, total, cot_ref, last_inner, last_outer, scale):
    piece = last_inner.shape[0]
    last = jnp.where(is_inner(z), last_inner[...], last_outer[...])
    total = total + jnp.dot(cot_ref[:, 3 * piece :], last, preferred_element_type=jnp.float32)
    return (scale * total).astype(jnp.bfloat16)


def early_kernel(where_ref, far_ref, cot_ref, own, beside, mid_inner, mid_outer, total_out):
    rows = far_ref.shape[0]
    for n, ref in enumerate((far_ref, cot_ref.at[3 * rows // 2 : 5 * rows // 2])):

        @pl.when(pl.program_id(0) == n)
        def _(ref=ref):
            total_out[...] = near_sum(where_ref[0], ref, own, beside, mid_inner, mid_outer)


def send_kernel(scale, where_ref, far_ref, cot_ref, total_ref, last_inner, last_outer, up_out, down_out):
    rows = far_ref.shape[0]
    half = rows // 2
    for n, ref in enumerate((far_ref, cot_ref.at[3 * half : 5 * half])):
        to = slice(n * half, (n + 1) * half)
        value = with_last(where_ref[0], total_ref[n * rows : (n + 1) * rows], ref, last_inner, last_outer, scale)
        up_out[to] = value[:half]
        down_out[to] = value[half:]


def near_kernel(scale, where_ref, cot_ref, own, beside, mid_inner, mid_outer, last_inner, last_outer, *outs):
    z = where_ref[0]
    total = near_sum(z, cot_ref, own, beside, mid_inner, mid_outer)
    value = with_last(z, total, cot_ref, last_inner, last_outer, scale)
    for n, out_ref in enumerate(outs):

        @pl.when(pl.program_id(0) == n)
        def _(out_ref=out_ref):
            out_ref[...] = value


def rows_kernel(body, steps, ins, out, outs, kind, limit, cost, name, where, *arrays):
    whole = lambda shape: pl.BlockSpec(shape, lambda i: (0, 0))
    return pl.pallas_call(
        body,
        grid=(steps,),
        out_shape=[jax.ShapeDtypeStruct(shape, kind) for shape in outs],
        in_specs=[SMEM] + [ins.get(n) or whole(value.shape) for n, value in enumerate(arrays)],
        out_specs=[out or whole(shape) for shape in outs],
        compiler_params=pltpu.CompilerParams(vmem_limit_bytes=limit * 2**20),
        cost_estimate=pl.CostEstimate(flops=cost, bytes_accessed=2**20, transcendentals=0),
        name=name,
    )(where, *arrays)


def finish_kernel(gate_ref, up_ref, own_top, own_low, top_up, low_up, top_down, low_down, gate_out, up_out):
    def write(own, first, second):
        grad = own[...].astype(jnp.float32) + first[...].astype(jnp.float32) + second[...].astype(jnp.float32)
        gate = gate_ref[...].astype(jnp.float32)
        sig = jax.nn.sigmoid(gate)
        gate_out[...] = (grad * up_ref[...].astype(jnp.float32) * sig * (1.0 + gate * (1.0 - sig))).astype(jnp.bfloat16)
        up_out[...] = (grad * (gate * sig)).astype(jnp.bfloat16)

    @pl.when(pl.program_id(0) == 0)
    def _():
        write(own_top, top_up, top_down)

    @pl.when(pl.program_id(0) == 1)
    def _():
        write(own_low, low_up, low_down)


def finish(gate, up, *terms):
    rows, width = gate.shape
    block = pl.BlockSpec((rows // 2, width), lambda i: (i, 0))
    whole = pl.BlockSpec((rows // 2, width), lambda i: (0, 0))
    second = pl.BlockSpec((rows // 2, width), lambda i: (1, 0))
    return pl.pallas_call(
        finish_kernel,
        grid=(2,),
        out_shape=[jax.ShapeDtypeStruct((rows, width), jnp.bfloat16)] * 2,
        in_specs=[block, block] + [whole] * 3 + [second] * 2 + [whole],
        out_specs=[block, block],
        compiler_params=pltpu.CompilerParams(vmem_limit_bytes=16 * 2**20),
        cost_estimate=pl.CostEstimate(flops=10 * rows * width, bytes_accessed=14 * rows * width, transcendentals=rows * width),
        name="finish",
    )(gate, up, *terms)


def tie(*values):
    return lax.optimization_barrier(values)


def turn(value, by):
    return lax.ppermute(value, "x", [(i, (i + by) % SIDE) for i in range(SIDE)])


def on_line(value, pairs):
    return lax.ppermute(value, "z", pairs)


BESIDE = [(0, 1), (1, 0), (2, 3), (3, 2)]
INNER = [(1, 2), (2, 1)]
OUTWARD = [(1, 0), (2, 3)]
INWARD = [(0, 1), (3, 2)]


def add(a, b):
    return (a.astype(jnp.float32) + b.astype(jnp.float32)).astype(jnp.bfloat16)


def local(theta_outer, theta_local, momentum, gate_pre, up_pre, cotangent, partner, chosen):
    outer, local_rows, moment = theta_outer[0], theta_local[0], momentum[0]
    rows, width = outer.shape
    scale = width ** (-0.5)
    z, x = lax.axis_index("z"), lax.axis_index("x")
    my_rep = lax.axis_index("rep")
    replicas = lax.axis_size("rep")
    offset = jnp.bitwise_xor(partner[0, my_rep], my_rep)

    def to_partner(by):
        return lambda value: lax.ppermute(value, "rep", [(i, i ^ by) for i in range(replicas)])

    where = jnp.stack([z, x]).astype(jnp.int32)
    gate, upper = gate_pre[0], up_pre[0]
    picked, hidden, cot_own, go_up, go_down = prepare(where, chosen, outer, local_rows, gate, upper, cotangent[0])
    go_up, go_down = turn(go_up, 1), turn(go_down, -1)

    moved = lax.switch(offset - 1, [to_partner(by) for by in range(1, replicas)], picked)
    momentum_new, theta_new = outer_step(chosen, outer, local_rows, moment, moved)
    beside, last_inner = on_line(theta_new, BESIDE), on_line(theta_new, INNER)
    far = width + cot_own.shape[1]
    last_up, last_down = turn(go_up[:, :far], 1), turn(go_down[:, :far], -1)

    cot, hid = gather_near(hidden, cot_own, go_up, go_down)
    beside, last_inner, cot, hid = tie(beside, last_inner, cot, hid)
    mid_inner, mid_outer = on_line(beside, INNER), on_line(last_inner, OUTWARD)
    cot_far, part3, part2, part1, part_own = weight_parts(scale, cot, hid, last_up, last_down)
    third = on_line(part3, INWARD)
    mid_inner, mid_outer = tie(mid_inner, mid_outer)
    last_outer = on_line(mid_inner, OUTWARD)
    half, depth = rows // 2, cot.shape[1]
    early = (theta_new, beside, mid_inner, mid_outer)
    (total,) = rows_kernel(
        early_kernel, 2, {}, pl.BlockSpec((rows, width), lambda i: (i, 0)), [(2 * rows, width)], jnp.float32, 32, 2**20,
        "early_rows", where, cot_far, cot, *early,
    )
    third, part2 = tie(third, part2)
    third, second = on_line(add(part2, third), INNER), on_line(part2, INWARD)

    far_up, far_down = rows_kernel(
        functools.partial(send_kernel, scale), 1, {}, None, [(rows, width)] * 2, jnp.bfloat16, 24, 2**20,
        "send_rows", where, cot_far, cot, total, last_inner, last_outer,
    )
    far_up, far_down = turn(far_up, 1), turn(far_down, -1)
    chunk = pl.BlockSpec((half, depth), lambda i: (jnp.where(i < 2, 2 + 3 * i, i - 2), 0))
    up_add, down_add, own_top, own_low = rows_kernel(
        functools.partial(near_kernel, scale), 4, {0: chunk}, None, [(half, width)] * 4, jnp.bfloat16, 32,
        8 * half * depth * width, "other_rows", where, cot, *early, last_inner, last_outer,
    )

    first, second = on_line(add(part1, third), BESIDE), on_line(add(part3, second), INNER)
    up_add, down_add = add(up_add, far_up[:half]), add(down_add, far_down[:half])
    top_up, low_down = turn(up_add, 1), turn(down_add, -1)
    grad_weight = part_own.astype(jnp.float32) + first.astype(jnp.float32) + second.astype(jnp.float32)
    grad_gate, grad_up = finish(gate, upper, own_top, own_low, top_up, far_up, far_down, low_down)
    return momentum_new[None], grad_weight.astype(jnp.bfloat16)[None], grad_gate[None], grad_up[None]


def solution(mesh):
    replicas, shards = mesh.devices.shape
    grid = Mesh(mesh.devices.reshape(replicas, shards // SIDE, SIDE), ("rep", "z", "x"))
    rows = P("rep", ("z", "x"), None)
    per_shard = P(("z", "x"), None)
    return jax.shard_map(
        local,
        mesh=grid,
        in_specs=(rows,) * 6 + (per_shard,) * 2,
        out_specs=(rows,) * 4,
        check_vma=False,
    )
```

profile of v0, /device:TPU:6, one launch (start us, length us, event | category | flops | bytes accessed | tf_op | source)
XLA Modules:
  0.0 152.7 jit_solution(4159166937873351823)
XLA Ops:
  0.6 0.0 copy-start
  0.7 0.7 pad_add_fusion.where_ref
  1.3 5.8 %prepare.1 = (bf16[14,128,128]{2,1,0:T(8,128)(2,1)}, bf16[2,128,1792]{2,1,0:T(8,128)(2,1)}, bf16[2,128,1024]{2,1,0:T(8,128)(2,1)}, bf16[128,6656]{1,0:T(8,128)(2,1)}, bf16[128,6656]{1,0:T(8,128)(2,1)}) custom-call(s32[2]{0:T(128)} %pad_add_fusion.where_ref, s32[1,14]{1,0:T(1,128)} %chosen_ref.3, bf16[2,128,1792]{2,1,0:T(8,128)(2,1)} %bitcast.26, ...), custom_call_target="tpu_custom_call" | custom-call | flops 1835008 | bytes 11534336 | tf_op jit(solution)/shard_map/prepare/pallas_call | solution.py:109
  7.1 2.2 %collective-permute-start.17 = (bf16[128,6656]{1,0:T(8,128)(2,1)}, bf16[128,6656]{1,0:T(8,128)(2,1)S(1)}, u32[]{:S(2)}, u32[]{:S(2)}) collective-permute-start(bf16[128,6656]{1,0:T(8,128)(2,1)} %get-tuple-element.70), channel_id=1, source_target_pairs={{0,1},{1,2},{2,3},{3,0},{4,5},{5,6},{6,7},{7,4},{8,9},{9,10},{10,1... | collective-permute-start | bytes 5111816 | tf_op jit(solution)/shard_map/ppermute | solution.py:298
  9.3 0.0 collective-permute-start.18
  9.3 0.0 copy-done
  9.3 0.6 constant_dynamic-slice_fusion
  10.5 11.9 %conditional.1 = (bf16[14,128,128]{2,1,0:T(8,128)(2,1)}) conditional(s32[]{:T(128)} %clamp.3, bf16[14,128,128]{2,1,0:T(8,128)(2,1)} %get-tuple-element.65, bf16[14,128,128]{2,1,0:T(8,128)(2,1)} %get-tuple-element.65, bf16[14,128,128]{2,1,0:T(8,128)(2,1)} %get-tuple-element.65, ...), branch_computations={%region_0.0_spmd, %region_1.0_spmd, %region_2.0_spmd, %region_3.0_... | conditional | bytes 1835056 | solution.py:332
  10.6 1.5 collective-permute-start.3
  12.0 10.4 %collective-permute-done.3 = bf16[14,128,128]{2,1,0:T(8,128)(2,1)} collective-permute-done((bf16[14,128,128]{2,1,0:T(8,128)(2,1)}, bf16[14,128,128]{2,1,0:T(8,128)(2,1)}, u32[]{:S(2)}, u32[]{:S(2)}) %collective-permute-start.3) | collective-permute-done | bytes 458784 | tf_op jit(solution)/shard_map/cond/branch_3_fun/ppermute | solution.py:325
  22.5 5.0 %outer_step.1 = (f32[256,1792]{1,0:T(8,128)}, bf16[256,1792]{1,0:T(8,128)(2,1)}) custom-call(s32[1,14]{1,0:T(1,128)} %chosen_ref.3, bf16[256,1792]{1,0:T(8,128)(2,1)} %bitcast.27, bf16[256,1792]{1,0:T(8,128)(2,1)} %bitcast.29, f32[256,1792]{1,0:T(8,128)} %bitcast.31, bf16[14,128,128]{2,1,0:T(8,128)(2,1)} %get-tuple-element.95.moved_ref), custom_call_target="tpu_custom_call" | custom-call | flops 3670016 | bytes 6422528 | tf_op jit(solution)/shard_map/outer_step/pallas_call | solution.py:47
  27.4 0.9 collective-permute-start.16
  28.3 17.6 %collective-permute-start.15 = (bf16[256,1792]{1,0:T(8,128)(2,1)}, bf16[256,1792]{1,0:T(8,128)(2,1)S(1)}, u32[]{:S(2)}, u32[]{:S(2)}) collective-permute-start(bf16[256,1792]{1,0:T(8,128)(2,1)} %get-tuple-element.67.own), channel_id=1, source_target_pairs={{0,4},{4,0},{8,12},{12,8},{1,5},{5,1},{9,13},{13,9},{2,6},{6,2},{1... | collective-permute-start | bytes 2752520 | tf_op jit(solution)/shard_map/ppermute | solution.py:302
  45.9 0.3 collective-permute-done.17.go_up
  46.3 1.8 %collective-permute-start.19 = (bf16[128,2816]{1,0:T(8,128)(2,1)S(1)}, bf16[128,2816]{1,0:T(8,128)(2,1)S(1)}, u32[]{:S(2)}, u32[]{:S(2)}) collective-permute-start(bf16[128,2816]{1,0:T(8,128)(2,1)S(1)} %slice.16), channel_id=1, source_target_pairs={{0,1},{1,2},{2,3},{3,0},{4,5},{5,6},{6,7},{7,4},{8,9},{9,10},{10,1... | collective-permute-start | bytes 2162696 | tf_op jit(solution)/shard_map/ppermute | solution.py:298
  48.0 0.0 collective-permute-done.18.go_down
  48.1 0.6 collective-permute-start.20
  48.7 0.0 copy-done.4
  48.7 0.0 copy-done.5
  48.7 0.3 gather_near.1
  49.0 0.0 collective-permute-done.16.last_inner
  49.0 16.2 %collective-permute-done.15.beside = bf16[256,1792]{1,0:T(8,128)(2,1)S(1)} collective-permute-done((bf16[256,1792]{1,0:T(8,128)(2,1)}, bf16[256,1792]{1,0:T(8,128)(2,1)S(1)}, u32[]{:S(2)}, u32[]{:S(2)}) %collective-permute-start.15) | collective-permute-done | bytes 917536 | tf_op jit(solution)/shard_map/ppermute | solution.py:302
  65.2 0.7 collective-permute-start.26
  66.0 1.3 collective-permute-start.27
  67.3 0.0 collective-permute-done.19.last_up
  67.3 0.9 collective-permute-done.20.last_down
  68.2 4.8 %weight_parts.1 = (bf16[256,1024]{1,0:T(8,128)(2,1)S(1)}, bf16[256,1792]{1,0:T(8,128)(2,1)S(1)}, bf16[256,1792]{1,0:T(8,128)(2,1)S(1)}, bf16[256,1792]{1,0:T(8,128)(2,1)S(1)}, bf16[256,1792]{1,0:T(8,128)(2,1)S(1)}) custom-call(bf16[768,1024]{1,0:T(8,128)(2,1)S(1)} %get-tuple-element.74.cot.cot_ref, bf16[768,1792]{1,0:T(8,128)(2,1)S(1)} %get-tuple-element.75.hid, ...), custom_call_target="tpu_custom_call" | custom-call | flops 1048576 | bytes 1048576 | tf_op jit(solution)/shard_map/weight_parts/pallas_call | solution.py:182
  73.0 0.0 copy-start.1
  73.0 0.0 copy-start.6
  73.0 5.9 %collective-permute-start.21 = (bf16[256,1792]{1,0:T(8,128)(2,1)S(1)}, bf16[256,1792]{1,0:T(8,128)(2,1)S(1)}, u32[]{:S(2)}, u32[]{:S(2)}) collective-permute-start(bf16[256,1792]{1,0:T(8,128)(2,1)S(1)} %get-tuple-element.78), channel_id=1, source_target_pairs={{0,4},{12,8},{1,5},{13,9},{2,6},{14,10},{3,7},{15,11},{16,20},{28,... | collective-permute-start | bytes 2752520 | tf_op jit(solution)/shard_map/ppermute | solution.py:302
  78.9 0.0 collective-permute-done.26.mid_inner
  78.9 10.6 %collective-permute-done.27.mid_outer = bf16[256,1792]{1,0:T(8,128)(2,1)S(1)} collective-permute-done((bf16[256,1792]{1,0:T(8,128)(2,1)S(1)}, bf16[256,1792]{1,0:T(8,128)(2,1)S(1)}, u32[]{:S(2)}, u32[]{:S(2)}) %collective-permute-start.27) | collective-permute-done | bytes 917536 | tf_op jit(solution)/shard_map/ppermute | solution.py:302
  89.5 1.3 collective-permute-start.28
  90.8 4.9 %collective-permute-done.21 = bf16[256,1792]{1,0:T(8,128)(2,1)S(1)} collective-permute-done((bf16[256,1792]{1,0:T(8,128)(2,1)S(1)}, bf16[256,1792]{1,0:T(8,128)(2,1)S(1)}, u32[]{:S(2)}, u32[]{:S(2)}) %collective-permute-start.21) | collective-permute-done | bytes 917536 | tf_op jit(solution)/shard_map/ppermute | solution.py:302
  95.7 0.2 add_convert_fusion.3
  96.0 0.7 collective-permute-start.22
  96.7 6.2 %collective-permute-start.24 = (bf16[256,1792]{1,0:T(8,128)(2,1)S(1)}, bf16[256,1792]{1,0:T(8,128)(2,1)S(1)}, u32[]{:S(2)}, u32[]{:S(2)}) collective-permute-start(bf16[256,1792]{1,0:T(8,128)(2,1)S(1)} %get-tuple-element.80), channel_id=1, source_target_pairs={{0,4},{12,8},{1,5},{13,9},{2,6},{14,10},{3,7},{15,11},{16,20},{28,... | collective-permute-start | bytes 2752520 | tf_op jit(solution)/shard_map/ppermute | solution.py:302
  102.9 0.0 copy-done.1
  102.9 2.4 %early_rows.1.total_ref = f32[512,1792]{1,0:T(8,128)S(1)} custom-call(s32[2]{0:T(128)S(1)} %copy-done.6, bf16[256,1024]{1,0:T(8,128)(2,1)S(1)} %get-tuple-element.89.far_ref, bf16[768,1024]{1,0:T(8,128)(2,1)S(1)} %get-tuple-element.74.cot.cot_ref, bf16[256,1792]{1,0:T(8,128)(2,1)S(1)} %copy-done.1, bf16[256,1792]{1,0:T(8,128)(2,1)S(1)} %collective-permute-done.15.beside, ...), custom_call_target="tpu_custom_call" | custom-call | flops 1048576 | bytes 1048576 | tf_op jit(solution)/shard_map/early_rows/pallas_call | solution.py:247
  105.3 4.8 %collective-permute-done.28.last_outer = bf16[256,1792]{1,0:T(8,128)(2,1)S(1)} collective-permute-done((bf16[256,1792]{1,0:T(8,128)(2,1)S(1)}, bf16[256,1792]{1,0:T(8,128)(2,1)S(1)}, u32[]{:S(2)}, u32[]{:S(2)}) %collective-permute-start.28) | collective-permute-done | bytes 917536 | tf_op jit(solution)/shard_map/ppermute | solution.py:302
  110.1 1.2 send_rows.1
  111.4 0.1 collective-permute-start.29
  111.4 2.0 %collective-permute-start.31 = (bf16[256,1792]{1,0:T(8,128)(2,1)S(1)}, bf16[256,1792]{1,0:T(8,128)(2,1)S(1)}, u32[]{:S(2)}, u32[]{:S(2)}) collective-permute-start(bf16[256,1792]{1,0:T(8,128)(2,1)S(1)} %get-tuple-element.91), channel_id=1, source_target_pairs={{0,3},{1,0},{2,1},{3,2},{4,7},{5,4},{6,5},{7,6},{8,11},{9,8},{10,9... | collective-permute-start | bytes 2752520 | tf_op jit(solution)/shard_map/ppermute | solution.py:298
  113.5 3.5 %other_rows.1 = (bf16[128,1792]{1,0:T(8,128)(2,1)S(1)}, bf16[128,1792]{1,0:T(8,128)(2,1)S(1)}, bf16[128,1792]{1,0:T(8,128)(2,1)S(1)}, bf16[128,1792]{1,0:T(8,128)(2,1)S(1)}) custom-call(s32[2]{0:T(128)S(1)} %copy-done.6, bf16[768,1024]{1,0:T(8,128)(2,1)S(1)} %get-tuple-element.74.cot.cot_ref, bf16[256,1792]{1,0:T(8,128)(2,1)S(1)} %copy-done.1, ...), custom_call_target="tpu_custom_call" | custom-call | flops 1879048192 | bytes 1048576 | tf_op jit(solution)/shard_map/other_rows/pallas_call | solution.py:247
  117.0 0.0 collective-permute-done.22
  117.0 0.2 add_convert_fusion.2
  117.2 1.9 %collective-permute-start.23 = (bf16[256,1792]{1,0:T(8,128)(2,1)S(1)}, bf16[256,1792]{1,0:T(8,128)(2,1)S(1)}, u32[]{:S(2)}, u32[]{:S(2)}) collective-permute-start(bf16[256,1792]{1,0:T(8,128)(2,1)S(1)} %add_convert_fusion.2), channel_id=1, source_target_pairs={{0,4},{4,0},{8,12},{12,8},{1,5},{5,1},{9,13},{13,9},{2,6},{6,2},{1... | collective-permute-start | bytes 2752520 | tf_op jit(solution)/shard_map/ppermute | solution.py:302
  119.1 3.9 %collective-permute-done.24 = bf16[256,1792]{1,0:T(8,128)(2,1)S(1)} collective-permute-done((bf16[256,1792]{1,0:T(8,128)(2,1)S(1)}, bf16[256,1792]{1,0:T(8,128)(2,1)S(1)}, u32[]{:S(2)}, u32[]{:S(2)}) %collective-permute-start.24) | collective-permute-done | bytes 917536 | tf_op jit(solution)/shard_map/ppermute | solution.py:302
  123.0 0.2 add_convert_fusion.1
  123.2 0.0 copy-start.2
  123.2 0.0 copy-start.3
  123.3 0.9 collective-permute-start.25
  124.1 5.1 %collective-permute-done.29.low_up = bf16[256,1792]{1,0:T(8,128)(2,1)S(1)} collective-permute-done((bf16[256,1792]{1,0:T(8,128)(2,1)S(1)}, bf16[256,1792]{1,0:T(8,128)(2,1)S(1)}, u32[]{:S(2)}, u32[]{:S(2)}) %collective-permute-start.29) | collective-permute-done | bytes 917536 | tf_op jit(solution)/shard_map/ppermute | solution.py:298
  129.2 0.1 add_convert_fusion.5
  129.3 10.0 %collective-permute-start.30 = (bf16[128,1792]{1,0:T(8,128)(2,1)S(1)}, bf16[128,1792]{1,0:T(8,128)(2,1)S(1)}, u32[]{:S(2)}, u32[]{:S(2)}) collective-permute-start(bf16[128,1792]{1,0:T(8,128)(2,1)S(1)} %add_convert_fusion.5), channel_id=1, source_target_pairs={{0,1},{1,2},{2,3},{3,0},{4,5},{5,6},{6,7},{7,4},{8,9},{9,10},{10,1... | collective-permute-start | bytes 1376264 | tf_op jit(solution)/shard_map/ppermute | solution.py:298
  139.3 0.0 collective-permute-done.31.top_down
  139.3 0.1 add_convert_fusion.4
  139.4 0.1 collective-permute-start.32
  139.5 7.0 %collective-permute-done.30.top_up = bf16[128,1792]{1,0:T(8,128)(2,1)S(1)} collective-permute-done((bf16[128,1792]{1,0:T(8,128)(2,1)S(1)}, bf16[128,1792]{1,0:T(8,128)(2,1)S(1)}, u32[]{:S(2)}, u32[]{:S(2)}) %collective-permute-start.30) | collective-permute-done | bytes 458784 | tf_op jit(solution)/shard_map/ppermute | solution.py:298
  146.5 2.8 %collective-permute-done.32.low_down = bf16[128,1792]{1,0:T(8,128)(2,1)S(1)} collective-permute-done((bf16[128,1792]{1,0:T(8,128)(2,1)S(1)}, bf16[128,1792]{1,0:T(8,128)(2,1)S(1)}, u32[]{:S(2)}, u32[]{:S(2)}) %collective-permute-start.32) | collective-permute-done | bytes 458784 | tf_op jit(solution)/shard_map/ppermute | solution.py:298
  149.3 2.1 %finish.1 = (bf16[256,1792]{1,0:T(8,128)(2,1)}, bf16[256,1792]{1,0:T(8,128)(2,1)}) custom-call(bf16[256,1792]{1,0:T(8,128)(2,1)S(1)} %bitcast.21, bf16[256,1792]{1,0:T(8,128)(2,1)S(1)} %bitcast.23, bf16[128,1792]{1,0:T(8,128)(2,1)S(1)} %get-tuple-element.86.own_top, bf16[128,1792]{1,0:T(8,128)(2,1)S(1)} %get-tuple-element.87.own_low, ...), custom_call_target="tpu_custom_call" | custom-call | flops 4587520 | bytes 6422528 | tf_op jit(solution)/shard_map/finish/pallas_call | solution.py:281
  151.4 0.0 collective-permute-done.23
  151.4 0.0 collective-permute-done.25
  151.4 1.3 fusion
  (7 shorter events, 0.1 us)
Async XLA Ops:
  0.6 8.7 %copy-start = (s32[1,16]{1,0:T(1,128)S(1)}, s32[1,16]{1,0:T(1,128)}, u32[]{:S(2)}) copy-start(s32[1,16]{1,0:T(1,128)} %param.29) | copy-start | bytes 196
  7.1 39.2 %collective-permute-start.17 = (bf16[128,6656]{1,0:T(8,128)(2,1)}, bf16[128,6656]{1,0:T(8,128)(2,1)S(1)}, u32[]{:S(2)}, u32[]{:S(2)}) collective-permute-start(bf16[128,6656]{1,0:T(8,128)(2,1)} %get-tuple-element.70), channel_id=1, source_target_pairs={{0,1},{1,2},{2,3},{3,0},{4,5},{5,6},{6,7},{7,4},{8,9},{9,10},{10,1... | collective-permute-start | bytes 5111816 | tf_op jit(solution)/shard_map/ppermute | solution.py:298
  9.3 38.7 %collective-permute-start.18 = (bf16[128,6656]{1,0:T(8,128)(2,1)}, bf16[128,6656]{1,0:T(8,128)(2,1)S(1)}, u32[]{:S(2)}, u32[]{:S(2)}) collective-permute-start(bf16[128,6656]{1,0:T(8,128)(2,1)} %get-tuple-element.71), channel_id=1, source_target_pairs={{0,3},{1,0},{2,1},{3,2},{4,7},{5,4},{6,5},{7,6},{8,11},{9,8},{10,9... | collective-permute-start | bytes 5111816 | tf_op jit(solution)/shard_map/ppermute | solution.py:298
  10.6 11.9 %collective-permute-start.3 = (bf16[14,128,128]{2,1,0:T(8,128)(2,1)}, bf16[14,128,128]{2,1,0:T(8,128)(2,1)}, u32[]{:S(2)}, u32[]{:S(2)}) collective-permute-start(bf16[14,128,128]{2,1,0:T(8,128)(2,1)} %param.3), channel_id=1, source_target_pairs={{0,64},{16,80},{32,96},{48,112},{64,0},{80,16},{96,32},{112,48},{1... | collective-permute-start | bytes 1376264 | tf_op jit(solution)/shard_map/cond/branch_3_fun/ppermute | solution.py:325
  27.4 21.3 %copy-start.4 = (bf16[2,128,1792]{2,1,0:T(8,128)(2,1)S(1)}, bf16[2,128,1792]{2,1,0:T(8,128)(2,1)}, u32[]{:S(2)}) copy-start(bf16[2,128,1792]{2,1,0:T(8,128)(2,1)} %get-tuple-element.68) | copy-start | bytes 2752516
  27.4 21.3 %copy-start.5 = (bf16[2,128,1024]{2,1,0:T(8,128)(2,1)S(1)}, bf16[2,128,1024]{2,1,0:T(8,128)(2,1)}, u32[]{:S(2)}) copy-start(bf16[2,128,1024]{2,1,0:T(8,128)(2,1)} %get-tuple-element.69) | copy-start | bytes 1572868
  27.4 21.6 %collective-permute-start.16 = (bf16[256,1792]{1,0:T(8,128)(2,1)}, bf16[256,1792]{1,0:T(8,128)(2,1)S(1)}, u32[]{:S(2)}, u32[]{:S(2)}) collective-permute-start(bf16[256,1792]{1,0:T(8,128)(2,1)} %get-tuple-element.67.own), channel_id=1, source_target_pairs={{4,8},{8,4},{5,9},{9,5},{6,10},{10,6},{7,11},{11,7},{20,24},{24,20... | collective-permute-start | bytes 2752520 | tf_op jit(solution)/shard_map/ppermute | solution.py:302
  28.3 37.0 %collective-permute-start.15 = (bf16[256,1792]{1,0:T(8,128)(2,1)}, bf16[256,1792]{1,0:T(8,128)(2,1)S(1)}, u32[]{:S(2)}, u32[]{:S(2)}) collective-permute-start(bf16[256,1792]{1,0:T(8,128)(2,1)} %get-tuple-element.67.own), channel_id=1, source_target_pairs={{0,4},{4,0},{8,12},{12,8},{1,5},{5,1},{9,13},{13,9},{2,6},{6,2},{1... | collective-permute-start | bytes 2752520 | tf_op jit(solution)/shard_map/ppermute | solution.py:302
  46.3 21.0 %collective-permute-start.19 = (bf16[128,2816]{1,0:T(8,128)(2,1)S(1)}, bf16[128,2816]{1,0:T(8,128)(2,1)S(1)}, u32[]{:S(2)}, u32[]{:S(2)}) collective-permute-start(bf16[128,2816]{1,0:T(8,128)(2,1)S(1)} %slice.16), channel_id=1, source_target_pairs={{0,1},{1,2},{2,3},{3,0},{4,5},{5,6},{6,7},{7,4},{8,9},{9,10},{10,1... | collective-permute-start | bytes 2162696 | tf_op jit(solution)/shard_map/ppermute | solution.py:298
  48.1 20.1 %collective-permute-start.20 = (bf16[128,2816]{1,0:T(8,128)(2,1)S(1)}, bf16[128,2816]{1,0:T(8,128)(2,1)S(1)}, u32[]{:S(2)}, u32[]{:S(2)}) collective-permute-start(bf16[128,2816]{1,0:T(8,128)(2,1)S(1)} %slice.17), channel_id=1, source_target_pairs={{0,3},{1,0},{2,1},{3,2},{4,7},{5,4},{6,5},{7,6},{8,11},{9,8},{10,9... | collective-permute-start | bytes 2162696 | tf_op jit(solution)/shard_map/ppermute | solution.py:298
  65.2 13.7 %collective-permute-start.26 = (bf16[256,1792]{1,0:T(8,128)(2,1)S(1)}, bf16[256,1792]{1,0:T(8,128)(2,1)S(1)}, u32[]{:S(2)}, u32[]{:S(2)}) collective-permute-start(bf16[256,1792]{1,0:T(8,128)(2,1)S(1)} %collective-permute-done.15.beside), channel_id=1, source_target_pairs={{4,8},{8,4},{5,9},{9,5},{6,10},{10,6},{7,11},{11,7},{20,24},{24,20... | collective-permute-start | bytes 2752520 | tf_op jit(solution)/shard_map/ppermute | solution.py:302
  66.0 23.6 %collective-permute-start.27 = (bf16[256,1792]{1,0:T(8,128)(2,1)S(1)}, bf16[256,1792]{1,0:T(8,128)(2,1)S(1)}, u32[]{:S(2)}, u32[]{:S(2)}) collective-permute-start(bf16[256,1792]{1,0:T(8,128)(2,1)S(1)} %collective-permute-done.16.last_inner), channel_id=1, source_target_pairs={{4,0},{8,12},{5,1},{9,13},{6,2},{10,14},{7,3},{11,15},{20,16},{24,... | collective-permute-start | bytes 2752520 | tf_op jit(solution)/shard_map/ppermute | solution.py:302
  73.0 29.9 %copy-start.1 = (bf16[256,1792]{1,0:T(8,128)(2,1)S(1)}, bf16[256,1792]{1,0:T(8,128)(2,1)}, u32[]{:S(2)}) copy-start(bf16[256,1792]{1,0:T(8,128)(2,1)} %get-tuple-element.67.own) | copy-start | bytes 2752516
  73.0 29.9 %copy-start.6 = (s32[2]{0:T(128)S(1)}, s32[2]{0:T(128)}, u32[]{:S(2)}) copy-start(s32[2]{0:T(128)} %pad_add_fusion.where_ref) | copy-start | bytes 28
  73.0 22.7 %collective-permute-start.21 = (bf16[256,1792]{1,0:T(8,128)(2,1)S(1)}, bf16[256,1792]{1,0:T(8,128)(2,1)S(1)}, u32[]{:S(2)}, u32[]{:S(2)}) collective-permute-start(bf16[256,1792]{1,0:T(8,128)(2,1)S(1)} %get-tuple-element.78), channel_id=1, source_target_pairs={{0,4},{12,8},{1,5},{13,9},{2,6},{14,10},{3,7},{15,11},{16,20},{28,... | collective-permute-start | bytes 2752520 | tf_op jit(solution)/shard_map/ppermute | solution.py:302
  89.5 20.6 %collective-permute-start.28 = (bf16[256,1792]{1,0:T(8,128)(2,1)S(1)}, bf16[256,1792]{1,0:T(8,128)(2,1)S(1)}, u32[]{:S(2)}, u32[]{:S(2)}) collective-permute-start(bf16[256,1792]{1,0:T(8,128)(2,1)S(1)} %collective-permute-done.26.mid_inner), channel_id=1, source_target_pairs={{4,0},{8,12},{5,1},{9,13},{6,2},{10,14},{7,3},{11,15},{20,16},{24,... | collective-permute-start | bytes 2752520 | tf_op jit(solution)/shard_map/ppermute | solution.py:302
  96.0 21.0 %collective-permute-start.22 = (bf16[256,1792]{1,0:T(8,128)(2,1)S(1)}, bf16[256,1792]{1,0:T(8,128)(2,1)S(1)}, u32[]{:S(2)}, u32[]{:S(2)}) collective-permute-start(bf16[256,1792]{1,0:T(8,128)(2,1)S(1)} %add_convert_fusion.3), channel_id=1, source_target_pairs={{4,8},{8,4},{5,9},{9,5},{6,10},{10,6},{7,11},{11,7},{20,24},{24,20... | collective-permute-start | bytes 2752520 | tf_op jit(solution)/shard_map/ppermute | solution.py:302
  96.7 26.3 %collective-permute-start.24 = (bf16[256,1792]{1,0:T(8,128)(2,1)S(1)}, bf16[256,1792]{1,0:T(8,128)(2,1)S(1)}, u32[]{:S(2)}, u32[]{:S(2)}) collective-permute-start(bf16[256,1792]{1,0:T(8,128)(2,1)S(1)} %get-tuple-element.80), channel_id=1, source_target_pairs={{0,4},{12,8},{1,5},{13,9},{2,6},{14,10},{3,7},{15,11},{16,20},{28,... | collective-permute-start | bytes 2752520 | tf_op jit(solution)/shard_map/ppermute | solution.py:302
  111.4 17.9 %collective-permute-start.29 = (bf16[256,1792]{1,0:T(8,128)(2,1)S(1)}, bf16[256,1792]{1,0:T(8,128)(2,1)S(1)}, u32[]{:S(2)}, u32[]{:S(2)}) collective-permute-start(bf16[256,1792]{1,0:T(8,128)(2,1)S(1)} %get-tuple-element.90), channel_id=1, source_target_pairs={{0,1},{1,2},{2,3},{3,0},{4,5},{5,6},{6,7},{7,4},{8,9},{9,10},{10,1... | collective-permute-start | bytes 2752520 | tf_op jit(solution)/shard_map/ppermute | solution.py:298
  111.4 27.9 %collective-permute-start.31 = (bf16[256,1792]{1,0:T(8,128)(2,1)S(1)}, bf16[256,1792]{1,0:T(8,128)(2,1)S(1)}, u32[]{:S(2)}, u32[]{:S(2)}) collective-permute-start(bf16[256,1792]{1,0:T(8,128)(2,1)S(1)} %get-tuple-element.91), channel_id=1, source_target_pairs={{0,3},{1,0},{2,1},{3,2},{4,7},{5,4},{6,5},{7,6},{8,11},{9,8},{10,9... | collective-permute-start | bytes 2752520 | tf_op jit(solution)/shard_map/ppermute | solution.py:298
  117.2 34.2 %collective-permute-start.23 = (bf16[256,1792]{1,0:T(8,128)(2,1)S(1)}, bf16[256,1792]{1,0:T(8,128)(2,1)S(1)}, u32[]{:S(2)}, u32[]{:S(2)}) collective-permute-start(bf16[256,1792]{1,0:T(8,128)(2,1)S(1)} %add_convert_fusion.2), channel_id=1, source_target_pairs={{0,4},{4,0},{8,12},{12,8},{1,5},{5,1},{9,13},{13,9},{2,6},{6,2},{1... | collective-permute-start | bytes 2752520 | tf_op jit(solution)/shard_map/ppermute | solution.py:302
  123.2 26.1 %copy-start.2 = (bf16[1,256,1792]{2,1,0:T(8,128)(2,1)S(1)}, bf16[1,256,1792]{2,1,0:T(8,128)(2,1)}, u32[]{:S(2)}) copy-start(bf16[1,256,1792]{2,1,0:T(8,128)(2,1)} %param.26) | copy-start | bytes 2752516
  123.2 26.0 %copy-start.3 = (bf16[1,256,1792]{2,1,0:T(8,128)(2,1)S(1)}, bf16[1,256,1792]{2,1,0:T(8,128)(2,1)}, u32[]{:S(2)}) copy-start(bf16[1,256,1792]{2,1,0:T(8,128)(2,1)} %param.27) | copy-start | bytes 2752516
  123.3 28.2 %collective-permute-start.25 = (bf16[256,1792]{1,0:T(8,128)(2,1)S(1)}, bf16[256,1792]{1,0:T(8,128)(2,1)S(1)}, u32[]{:S(2)}, u32[]{:S(2)}) collective-permute-start(bf16[256,1792]{1,0:T(8,128)(2,1)S(1)} %add_convert_fusion.1), channel_id=1, source_target_pairs={{4,8},{8,4},{5,9},{9,5},{6,10},{10,6},{7,11},{11,7},{20,24},{24,20... | collective-permute-start | bytes 2752520 | tf_op jit(solution)/shard_map/ppermute | solution.py:302
  129.3 17.2 %collective-permute-start.30 = (bf16[128,1792]{1,0:T(8,128)(2,1)S(1)}, bf16[128,1792]{1,0:T(8,128)(2,1)S(1)}, u32[]{:S(2)}, u32[]{:S(2)}) collective-permute-start(bf16[128,1792]{1,0:T(8,128)(2,1)S(1)} %add_convert_fusion.5), channel_id=1, source_target_pairs={{0,1},{1,2},{2,3},{3,0},{4,5},{5,6},{6,7},{7,4},{8,9},{9,10},{10,1... | collective-permute-start | bytes 1376264 | tf_op jit(solution)/shard_map/ppermute | solution.py:298
  139.4 9.9 %collective-permute-start.32 = (bf16[128,1792]{1,0:T(8,128)(2,1)S(1)}, bf16[128,1792]{1,0:T(8,128)(2,1)S(1)}, u32[]{:S(2)}, u32[]{:S(2)}) collective-permute-start(bf16[128,1792]{1,0:T(8,128)(2,1)S(1)} %add_convert_fusion.4), channel_id=1, source_target_pairs={{0,3},{1,0},{2,1},{3,2},{4,7},{5,4},{6,5},{7,6},{8,11},{9,8},{10,9... | collective-permute-start | bytes 1376264 | tf_op jit(solution)/shard_map/ppermute | solution.py:298
where the time goes:
time: 154 us; the launch traced here: 153 us
  waiting for transfers between devices  67.1 us (44%)
  starting transfers between devices  55.5 us (36%)
  Pallas kernels  25 us (16%)
  other arithmetic  2.77 us (2%)
  between operations  1.54 us (1%)
    ppermute x10, waiting for transfers between devices, on_line(): return lax.ppermute(value, 'z', pairs)  40.5 us
    ppermute x10, starting transfers between devices, on_line(): return lax.ppermute(value, 'z', pairs)  37.3 us
    ppermute x8, starting transfers between devices, turn(): return lax.ppermute(value, 'x', [(i, (i + by) % SIDE) for i in range(SIDE)])  16.7 us
    ppermute x8, waiting for transfers between devices, turn(): return lax.ppermute(value, 'x', [(i, (i + by) % SIDE) for i in range(SIDE)])  16.1 us
    ppermute x1, waiting for transfers between devices, to_partner(): lax.ppermute(value, 'rep', [(i, i ^ by) for i in range(replicas)])  10.4 us
    pallas_call x3, Pallas kernels, rows_kernel(): pl.pallas_call(body, grid=(steps,), out_shape=[jax.ShapeDtypeStruct(shape...  7.12 us
    pallas_call x1, Pallas kernels, prepare(): pl.pallas_call(prepare_kernel, grid=(half // step,), out_shape=[jax.Shape...  5.77 us
    pallas_call x1, Pallas kernels, outer_step(): pl.pallas_call(step_kernel, grid=(rows // TILE, 2), out_shape=[jax.ShapeD...  4.95 us
  transfers between devices with their start and end apart: 19, of which 11 were waited for; matrix products, arithmetic and copies ran while one was open for 1% of the time, Pallas kernels for 13%

commit v1 on v0

--- a/solution.py
+++ b/solution.py
@@ -17,9 +17,9 @@
 SMEM = pl.BlockSpec(memory_space=pltpu.SMEM)
 
 
-def step_kernel(chosen_ref, outer_ref, local_ref, moment_ref, moved_ref, moment_out, theta_out, place):
+def step_kernel(chosen_ref, outer_ref, local_ref, moment_ref, moved_ref, out_ref, place):
     across = outer_ref.shape[1] // TILE
-    first = (pl.program_id(0) * pl.num_programs(1) + pl.program_id(1)) * across
+    first = pl.program_id(0) * across
 
     @pl.when(first == 0)
     def _():
@@ -36,27 +36,26 @@
         other = moved_ref[jnp.maximum(found, 0)].astype(jnp.float32)
         mixed = jnp.where(found >= 0, 0.5 * (delta + other), delta)
         moment = OUTER_MU * moment_ref[at] + mixed
-        moment_out[at] = moment
-        theta_out[at] = (outer - OUTER_RATE * (mixed + OUTER_MU * moment)).astype(jnp.bfloat16)
-
-
-def outer_step(chosen, outer, local_rows, moment, moved):
+        if out_ref.dtype == jnp.bfloat16:
+            out_ref[at] = (outer - OUTER_RATE * (mixed + OUTER_MU * moment)).astype(jnp.bfloat16)
+        else:
+            out_ref[at] = moment
+
+
+def outer_step(kind, chosen, outer, local_rows, moment, moved):
     rows, width = outer.shape
-    block = pl.BlockSpec((TILE, width // 2), lambda i, j: (i, j))
-    tiles = pl.BlockSpec(moved.shape, lambda i, j: (0, 0, 0))
+    block = pl.BlockSpec((TILE, width), lambda i: (i, 0))
+    tiles = pl.BlockSpec(moved.shape, lambda i: (0, 0, 0))
     return pl.pallas_call(
         step_kernel,
-        grid=(rows // TILE, 2),
-        out_shape=[
-            jax.ShapeDtypeStruct((rows, width), jnp.float32),
-            jax.ShapeDtypeStruct((rows, width), jnp.bfloat16),
-        ],
+        grid=(rows // TILE,),
+        out_shape=jax.ShapeDtypeStruct((rows, width), kind),
         in_specs=[SMEM, block, block, block, tiles],
-        out_specs=[block, block],
+        out_specs=block,
         scratch_shapes=[pltpu.SMEM((rows // TILE * (width // TILE),), jnp.int32)],
         compiler_params=pltpu.CompilerParams(vmem_limit_bytes=ALL_VMEM),
-        cost_estimate=pl.CostEstimate(flops=8 * rows * width, bytes_accessed=14 * rows * width, transcendentals=0),
-        name="outer_step",
+        cost_estimate=pl.CostEstimate(flops=8 * rows * width, bytes_accessed=2**20, transcendentals=0),
+        name="new_weights" if kind == jnp.bfloat16 else "new_momentum",
     )(chosen, outer, local_rows, moment, moved)
 
 
@@ -102,7 +101,7 @@
     depth = arrays[-1].shape[1]
     half, across = rows // 2, depth // SIDE
     assert half == TILE
-    step = half // 4
+    step = half // 2
     halves = lambda n: pl.BlockSpec((2, step, n), lambda i: (0, i, 0))
     go = pl.BlockSpec((step, 2 * width + 3 * across), lambda i: (i, 0))
     shapes = [(chosen.shape[1], TILE, TILE), (2, half, width), (2, half, across)] + [(half, 2 * width + 3 * across)] * 2
@@ -330,13 +329,14 @@
     go_up, go_down = turn(go_up, 1), turn(go_down, -1)
 
     moved = lax.switch(offset - 1, [to_partner(by) for by in range(1, replicas)], picked)
-    momentum_new, theta_new = outer_step(chosen, outer, local_rows, moment, moved)
+    theta_new = outer_step(jnp.bfloat16, chosen, outer, local_rows, moment, moved)
     beside, last_inner = on_line(theta_new, BESIDE), on_line(theta_new, INNER)
     far = width + cot_own.shape[1]
     last_up, last_down = turn(go_up[:, :far], 1), turn(go_down[:, :far], -1)
 
     cot, hid = gather_near(hidden, cot_own, go_up, go_down)
-    beside, last_inner, cot, hid = tie(beside, last_inner, cot, hid)
+    momentum_new = outer_step(jnp.float32, chosen, outer, local_rows, moment, moved)
+    beside, last_inner, cot, hid, momentum_new = tie(beside, last_inner, cot, hid, momentum_new)
     mid_inner, mid_outer = on_line(beside, INNER), on_line(last_inner, OUTWARD)
     cot_far, part3, part2, part1, part_own = weight_parts(scale, cot, hid, last_up, last_down)
     third = on_line(part3, INWARD)

time: 154 us -> 150 us (0.974); the launches traced: 153 us -> 147 us
  starting transfers between devices: 55.5 us -> 40.7 us
  local copies, waits for them, and re-layouts: 0.72 us -> 4.72 us
  Pallas kernels: 25 us -> 28.6 us
    ppermute x8, waiting for transfers between devices: 16.1 us -> 38 us  [turn(): return lax.ppermute(value, 'x', [(i, (i + by) % SIDE) for i in range(SIDE)])]
    ppermute x10, waiting for transfers between devices: 40.5 us -> 20.2 us  [on_line(): return lax.ppermute(value, 'z', pairs)]
    ppermute x10, starting transfers between devices: 37.3 us -> 19.7 us  [on_line(): return lax.ppermute(value, 'z', pairs)]
    ppermute x1, starting transfers between devices: 1.47 us -> 6.98 us  [to_partner(): lax.ppermute(value, 'rep', [(i, i ^ by) for i in range(replicas)])]
    slice x2, local copies, waits for them, and re-layouts: 0.09 us -> 2.93 us  [local(): last_up, last_down = (turn(go_up[:, :far], 1), turn(go_down[:, :far], -1))]
    ppermute x8, starting transfers between devices: 16.7 us -> 14 us  [turn(): return lax.ppermute(value, 'x', [(i, (i + by) % SIDE) for i in range(SIDE)])]
    pallas_call x1 -> x2, Pallas kernels: 4.95 us -> 6.95 us  [outer_step(): pl.pallas_call(step_kernel, grid=(rows // TILE,), out_shape=jax.ShapeDtyp...]
  transfers between devices with their start and end apart: 19 -> 19, of which waited for: 11 -> 10; matrix products, arithmetic and copies ran while one was open for 1% -> 3% of each run, Pallas kernels for 13% -> 16%
where the time goes in v1:
time: 150 us; the launch traced here: 147 us
  waiting for transfers between devices  68.6 us (46%)
  starting transfers between devices  40.7 us (27%)
  Pallas kernels  28.6 us (19%)
  local copies, waits for them, and re-layouts  4.72 us (3%)
  other arithmetic  2.69 us (2%)
  between operations  1.54 us (1%)
    ppermute x8, waiting for transfers between devices, turn(): return lax.ppermute(value, 'x', [(i, (i + by) % SIDE) for i in range(SIDE)])  38 us
    ppermute x10, waiting for transfers between devices, on_line(): return lax.ppermute(value, 'z', pairs)  20.2 us
    ppermute x10, starting transfers between devices, on_line(): return lax.ppermute(value, 'z', pairs)  19.7 us
    ppermute x8, starting transfers between devices, turn(): return lax.ppermute(value, 'x', [(i, (i + by) % SIDE) for i in range(SIDE)])  14 us
    ppermute x1, waiting for transfers between devices, to_partner(): lax.ppermute(value, 'rep', [(i, i ^ by) for i in range(replicas)])  10.4 us
    pallas_call x3, Pallas kernels, rows_kernel(): pl.pallas_call(body, grid=(steps,), out_shape=[jax.ShapeDtypeStruct(shape...  7.13 us
    ppermute x1, starting transfers between devices, to_partner(): lax.ppermute(value, 'rep', [(i, i ^ by) for i in range(replicas)])  6.98 us
    pallas_call x2, Pallas kernels, outer_step(): pl.pallas_call(step_kernel, grid=(rows // TILE,), out_shape=jax.ShapeDtyp...  6.95 us
  transfers between devices with their start and end apart: 19, of which 10 were waited for; matrix products, arithmetic and copies ran while one was open for 3% of the time, Pallas kernels for 16%

profile of v1, /device:TPU:6, one launch (start us, length us, event | category | flops | bytes accessed | tf_op | source)
XLA Modules:
  0.0 146.9 jit_solution(15200839020770448167)
XLA Ops:
  0.6 0.0 copy-start
  0.7 0.6 pad_add_fusion.where_ref
  1.2 4.5 %prepare.1 = (bf16[14,128,128]{2,1,0:T(8,128)(2,1)S(1)}, bf16[2,128,1792]{2,1,0:T(8,128)(2,1)}, bf16[2,128,1024]{2,1,0:T(8,128)(2,1)}, bf16[128,6656]{1,0:T(8,128)(2,1)}, bf16[128,6656]{1,0:T(8,128)(2,1)}) custom-call(s32[2]{0:T(128)} %pad_add_fusion.where_ref, s32[1,14]{1,0:T(1,128)} %chosen_ref.5, bf16[2,128,1792]{2,1,0:T(8,128)(2,1)} %bitcast.26, ...), custom_call_target="tpu_custom_call" | custom-call | flops 1835008 | bytes 11534336 | tf_op jit(solution)/shard_map/prepare/pallas_call | solution.py:108
  5.8 2.2 %collective-permute-start.17 = (bf16[128,6656]{1,0:T(8,128)(2,1)}, bf16[128,6656]{1,0:T(8,128)(2,1)S(1)}, u32[]{:S(2)}, u32[]{:S(2)}) collective-permute-start(bf16[128,6656]{1,0:T(8,128)(2,1)} %get-tuple-element.67), channel_id=1, source_target_pairs={{0,1},{1,2},{2,3},{3,0},{4,5},{5,6},{6,7},{7,4},{8,9},{9,10},{10,1... | collective-permute-start | bytes 5111816 | tf_op jit(solution)/shard_map/ppermute | solution.py:297
  8.0 0.0 collective-permute-start.18
  8.0 0.6 constant_dynamic-slice_fusion
  9.2 17.4 %conditional.1 = (bf16[14,128,128]{2,1,0:T(8,128)(2,1)}) conditional(s32[]{:T(128)} %clamp.3, bf16[14,128,128]{2,1,0:T(8,128)(2,1)S(1)} %get-tuple-element.64, bf16[14,128,128]{2,1,0:T(8,128)(2,1)S(1)} %get-tuple-element.64, bf16[14,128,128]{2,1,0:T(8,128)(2,1)S(1)} %get-tuple-element.64, ...), branch_computations={%region_0.0_spmd, %region_1.0_spmd, %region_2.0_spmd, %region_3.0_... | conditional | bytes 1835056 | solution.py:331
  9.3 7.0 %collective-permute-start.6 = (bf16[14,128,128]{2,1,0:T(8,128)(2,1)S(1)}, bf16[14,128,128]{2,1,0:T(8,128)(2,1)}, u32[]{:S(2)}, u32[]{:S(2)}) collective-permute-start(bf16[14,128,128]{2,1,0:T(8,128)(2,1)S(1)} %param.6), channel_id=1, source_target_pairs={{0,112},{16,96},{32,80},{48,64},{64,48},{80,32},{96,16},{112,0},{1... | collective-permute-start | bytes 1376264 | tf_op jit(solution)/shard_map/cond/branch_6_fun/ppermute | solution.py:324
  16.2 10.4 %collective-permute-done.6 = bf16[14,128,128]{2,1,0:T(8,128)(2,1)} collective-permute-done((bf16[14,128,128]{2,1,0:T(8,128)(2,1)S(1)}, bf16[14,128,128]{2,1,0:T(8,128)(2,1)}, u32[]{:S(2)}, u32[]{:S(2)}) %collective-permute-start.6) | collective-permute-done | bytes 458784 | tf_op jit(solution)/shard_map/cond/branch_6_fun/ppermute | solution.py:324
  26.7 3.5 %new_weights.1.own = bf16[256,1792]{1,0:T(8,128)(2,1)} custom-call(s32[1,14]{1,0:T(1,128)} %chosen_ref.5, bf16[256,1792]{1,0:T(8,128)(2,1)} %bitcast.27, bf16[256,1792]{1,0:T(8,128)(2,1)} %bitcast.30, f32[256,1792]{1,0:T(8,128)} %bitcast.32, bf16[14,128,128]{2,1,0:T(8,128)(2,1)} %get-tuple-element.93.moved_ref), custom_call_target="tpu_custom_call" | custom-call | flops 3670016 | bytes 1048576 | tf_op jit(solution)/shard_map/new_weights/pallas_call | solution.py:49
  30.2 0.7 collective-permute-start.16
  30.9 0.4 collective-permute-start.15
  31.3 13.6 %collective-permute-done.17.go_up = bf16[128,6656]{1,0:T(8,128)(2,1)S(1)} collective-permute-done((bf16[128,6656]{1,0:T(8,128)(2,1)}, bf16[128,6656]{1,0:T(8,128)(2,1)S(1)}, u32[]{:S(2)}, u32[]{:S(2)}) %collective-permute-start.17) | collective-permute-done | bytes 1703968 | tf_op jit(solution)/shard_map/ppermute | solution.py:297
  44.9 0.9 slice.16
  45.8 1.5 %collective-permute-start.19 = (bf16[128,2816]{1,0:T(8,128)(2,1)}, bf16[128,2816]{1,0:T(8,128)(2,1)}, u32[]{:S(2)}, u32[]{:S(2)}) collective-permute-start(bf16[128,2816]{1,0:T(8,128)(2,1)} %slice.16), channel_id=1, source_target_pairs={{0,1},{1,2},{2,3},{3,0},{4,5},{5,6},{6,7},{7,4},{8,9},{9,10},{10,1... | collective-permute-start | bytes 2162696 | tf_op jit(solution)/shard_map/ppermute | solution.py:297
  47.3 0.0 collective-permute-done.18.go_down
  47.3 2.0 %slice.17 = bf16[128,2816]{1,0:T(8,128)(2,1)} slice(bf16[128,6656]{1,0:T(8,128)(2,1)} %collective-permute-done.18.go_down), slice={[0:128], [0:2816]} | slice | bytes 1441792 | tf_op jit(solution)/shard_map/slice | solution.py:335
  49.4 0.5 collective-permute-start.20
  49.9 3.4 %new_momentum.1 = f32[256,1792]{1,0:T(8,128)} custom-call(s32[1,14]{1,0:T(1,128)} %chosen_ref.5, bf16[256,1792]{1,0:T(8,128)(2,1)} %bitcast.28, bf16[256,1792]{1,0:T(8,128)(2,1)} %bitcast.31, f32[256,1792]{1,0:T(8,128)} %bitcast.33, bf16[14,128,128]{2,1,0:T(8,128)(2,1)} %get-tuple-element.93.moved_ref), custom_call_target="tpu_custom_call" | custom-call | flops 3670016 | bytes 1048576 | tf_op jit(solution)/shard_map/new_momentum/pallas_call | solution.py:49
  53.3 0.0 copy-done.5
  53.3 1.2 copy-done.4
  54.5 1.7 %gather_near.1 = (bf16[768,1024]{1,0:T(8,128)(2,1)S(1)}, bf16[768,1792]{1,0:T(8,128)(2,1)S(1)}) custom-call(bf16[256,1792]{1,0:T(8,128)(2,1)S(1)} %bitcast.24, bf16[256,1024]{1,0:T(8,128)(2,1)S(1)} %bitcast.25, bf16[128,6656]{1,0:T(8,128)(2,1)S(1)} %collective-permute-done.17.go_up, bf16[128,6656]{1,0:T(8,128)(2,1)} %collective-permute-done.18.go_down), custom_call_target="tpu_custom_call" | custom-call | flops 1048576 | bytes 1048576 | tf_op jit(solution)/shard_map/gather_near/pallas_call | solution.py:142
  56.2 0.0 collective-permute-done.16.last_inner
  56.3 0.0 collective-permute-done.15.beside
  56.3 0.7 collective-permute-start.26
  57.0 1.3 collective-permute-start.27
  58.3 5.0 %collective-permute-done.19.last_up = bf16[128,2816]{1,0:T(8,128)(2,1)} collective-permute-done((bf16[128,2816]{1,0:T(8,128)(2,1)}, bf16[128,2816]{1,0:T(8,128)(2,1)}, u32[]{:S(2)}, u32[]{:S(2)}) %collective-permute-start.19) | collective-permute-done | bytes 720928 | tf_op jit(solution)/shard_map/ppermute | solution.py:297
  63.3 3.2 %collective-permute-done.20.last_down = bf16[128,2816]{1,0:T(8,128)(2,1)} collective-permute-done((bf16[128,2816]{1,0:T(8,128)(2,1)}, bf16[128,2816]{1,0:T(8,128)(2,1)}, u32[]{:S(2)}, u32[]{:S(2)}) %collective-permute-start.20) | collective-permute-done | bytes 720928 | tf_op jit(solution)/shard_map/ppermute | solution.py:297
  66.5 6.1 %weight_parts.1 = (bf16[256,1024]{1,0:T(8,128)(2,1)S(1)}, bf16[256,1792]{1,0:T(8,128)(2,1)S(1)}, bf16[256,1792]{1,0:T(8,128)(2,1)S(1)}, bf16[256,1792]{1,0:T(8,128)(2,1)S(1)}, bf16[256,1792]{1,0:T(8,128)(2,1)S(1)}) custom-call(bf16[768,1024]{1,0:T(8,128)(2,1)S(1)} %get-tuple-element.72.cot.cot_ref, bf16[768,1792]{1,0:T(8,128)(2,1)S(1)} %get-tuple-element.73.hid, ...), custom_call_target="tpu_custom_call" | custom-call | flops 1048576 | bytes 1048576 | tf_op jit(solution)/shard_map/weight_parts/pallas_call | solution.py:181
  72.6 0.0 copy-start.1
  72.7 5.3 %collective-permute-start.21 = (bf16[256,1792]{1,0:T(8,128)(2,1)S(1)}, bf16[256,1792]{1,0:T(8,128)(2,1)S(1)}, u32[]{:S(2)}, u32[]{:S(2)}) collective-permute-start(bf16[256,1792]{1,0:T(8,128)(2,1)S(1)} %get-tuple-element.76), channel_id=1, source_target_pairs={{0,4},{12,8},{1,5},{13,9},{2,6},{14,10},{3,7},{15,11},{16,20},{28,... | collective-permute-start | bytes 2752520 | tf_op jit(solution)/shard_map/ppermute | solution.py:301
  78.0 0.0 collective-permute-done.26.mid_inner
  78.0 4.1 %collective-permute-done.27.mid_outer = bf16[256,1792]{1,0:T(8,128)(2,1)S(1)} collective-permute-done((bf16[256,1792]{1,0:T(8,128)(2,1)S(1)}, bf16[256,1792]{1,0:T(8,128)(2,1)S(1)}, u32[]{:S(2)}, u32[]{:S(2)}) %collective-permute-start.27) | collective-permute-done | bytes 917536 | tf_op jit(solution)/shard_map/ppermute | solution.py:301
  82.0 1.3 collective-permute-start.28
  83.3 12.1 %collective-permute-done.21 = bf16[256,1792]{1,0:T(8,128)(2,1)S(1)} collective-permute-done((bf16[256,1792]{1,0:T(8,128)(2,1)S(1)}, bf16[256,1792]{1,0:T(8,128)(2,1)S(1)}, u32[]{:S(2)}, u32[]{:S(2)}) %collective-permute-start.21) | collective-permute-done | bytes 917536 | tf_op jit(solution)/shard_map/ppermute | solution.py:301
  95.4 0.2 add_convert_fusion.3
  95.7 0.7 collective-permute-start.22
  96.4 7.5 %collective-permute-start.24 = (bf16[256,1792]{1,0:T(8,128)(2,1)S(1)}, bf16[256,1792]{1,0:T(8,128)(2,1)S(1)}, u32[]{:S(2)}, u32[]{:S(2)}) collective-permute-start(bf16[256,1792]{1,0:T(8,128)(2,1)S(1)} %get-tuple-element.78), channel_id=1, source_target_pairs={{0,4},{12,8},{1,5},{13,9},{2,6},{14,10},{3,7},{15,11},{16,20},{28,... | collective-permute-start | bytes 2752520 | tf_op jit(solution)/shard_map/ppermute | solution.py:301
  103.9 2.4 %early_rows.1.total_ref = f32[512,1792]{1,0:T(8,128)S(1)} custom-call(s32[2]{0:T(128)S(1)} %copy-done.6, bf16[256,1024]{1,0:T(8,128)(2,1)S(1)} %get-tuple-element.87.far_ref, bf16[768,1024]{1,0:T(8,128)(2,1)S(1)} %get-tuple-element.72.cot.cot_ref, bf16[256,1792]{1,0:T(8,128)(2,1)S(1)} %copy-done.1, bf16[256,1792]{1,0:T(8,128)(2,1)S(1)} %collective-permute-done.15.beside, ...), custom_call_target="tpu_custom_call" | custom-call | flops 1048576 | bytes 1048576 | tf_op jit(solution)/shard_map/early_rows/pallas_call | solution.py:246
  106.3 0.0 collective-permute-done.28.last_outer
  106.3 1.2 send_rows.1
  107.6 0.2 collective-permute-start.29
  107.8 7.4 %collective-permute-start.31 = (bf16[256,1792]{1,0:T(8,128)(2,1)S(1)}, bf16[256,1792]{1,0:T(8,128)(2,1)S(1)}, u32[]{:S(2)}, u32[]{:S(2)}) collective-permute-start(bf16[256,1792]{1,0:T(8,128)(2,1)S(1)} %get-tuple-element.89), channel_id=1, source_target_pairs={{0,3},{1,0},{2,1},{3,2},{4,7},{5,4},{6,5},{7,6},{8,11},{9,8},{10,9... | collective-permute-start | bytes 2752520 | tf_op jit(solution)/shard_map/ppermute | solution.py:297
  115.2 3.5 %other_rows.1 = (bf16[128,1792]{1,0:T(8,128)(2,1)S(1)}, bf16[128,1792]{1,0:T(8,128)(2,1)S(1)}, bf16[128,1792]{1,0:T(8,128)(2,1)S(1)}, bf16[128,1792]{1,0:T(8,128)(2,1)S(1)}) custom-call(s32[2]{0:T(128)S(1)} %copy-done.6, bf16[768,1024]{1,0:T(8,128)(2,1)S(1)} %get-tuple-element.72.cot.cot_ref, bf16[256,1792]{1,0:T(8,128)(2,1)S(1)} %copy-done.1, ...), custom_call_target="tpu_custom_call" | custom-call | flops 1879048192 | bytes 1048576 | tf_op jit(solution)/shard_map/other_rows/pallas_call | solution.py:246
  118.7 0.0 collective-permute-done.22
  118.7 0.2 add_convert_fusion.2
  118.9 0.9 collective-permute-start.23
  119.8 4.0 %collective-permute-done.24 = bf16[256,1792]{1,0:T(8,128)(2,1)S(1)} collective-permute-done((bf16[256,1792]{1,0:T(8,128)(2,1)S(1)}, bf16[256,1792]{1,0:T(8,128)(2,1)S(1)}, u32[]{:S(2)}, u32[]{:S(2)}) %collective-permute-start.24) | collective-permute-done | bytes 917536 | tf_op jit(solution)/shard_map/ppermute | solution.py:301
  123.9 0.2 add_convert_fusion.1
  124.1 0.0 copy-start.2
  124.1 0.0 copy-start.3
  124.1 0.9 collective-permute-start.25
  125.0 8.4 %collective-permute-done.29.low_up = bf16[256,1792]{1,0:T(8,128)(2,1)S(1)} collective-permute-done((bf16[256,1792]{1,0:T(8,128)(2,1)S(1)}, bf16[256,1792]{1,0:T(8,128)(2,1)S(1)}, u32[]{:S(2)}, u32[]{:S(2)}) %collective-permute-start.29) | collective-permute-done | bytes 917536 | tf_op jit(solution)/shard_map/ppermute | solution.py:297
  133.4 0.1 add_convert_fusion.5
  133.5 0.1 collective-permute-start.30
  133.6 0.0 collective-permute-done.31.top_down
  133.6 0.1 add_convert_fusion.4
  133.7 2.1 %collective-permute-start.32 = (bf16[128,1792]{1,0:T(8,128)(2,1)S(1)}, bf16[128,1792]{1,0:T(8,128)(2,1)S(1)}, u32[]{:S(2)}, u32[]{:S(2)}) collective-permute-start(bf16[128,1792]{1,0:T(8,128)(2,1)S(1)} %add_convert_fusion.4), channel_id=1, source_target_pairs={{0,3},{1,0},{2,1},{3,2},{4,7},{5,4},{6,5},{7,6},{8,11},{9,8},{10,9... | collective-permute-start | bytes 1376264 | tf_op jit(solution)/shard_map/ppermute | solution.py:297
  135.8 6.7 %collective-permute-done.30.top_up = bf16[128,1792]{1,0:T(8,128)(2,1)S(1)} collective-permute-done((bf16[128,1792]{1,0:T(8,128)(2,1)S(1)}, bf16[128,1792]{1,0:T(8,128)(2,1)S(1)}, u32[]{:S(2)}, u32[]{:S(2)}) %collective-permute-start.30) | collective-permute-done | bytes 458784 | tf_op jit(solution)/shard_map/ppermute | solution.py:297
  142.5 0.9 collective-permute-done.32.low_down
  143.5 2.1 %finish.1 = (bf16[256,1792]{1,0:T(8,128)(2,1)}, bf16[256,1792]{1,0:T(8,128)(2,1)}) custom-call(bf16[256,1792]{1,0:T(8,128)(2,1)S(1)} %bitcast.21, bf16[256,1792]{1,0:T(8,128)(2,1)S(1)} %bitcast.23, bf16[128,1792]{1,0:T(8,128)(2,1)S(1)} %get-tuple-element.84.own_top, bf16[128,1792]{1,0:T(8,128)(2,1)S(1)} %get-tuple-element.85.own_low, ...), custom_call_target="tpu_custom_call" | custom-call | flops 4587520 | bytes 6422528 | tf_op jit(solution)/shard_map/finish/pallas_call | solution.py:280
  145.6 0.0 collective-permute-done.23
  145.6 0.0 collective-permute-done.25
  145.6 1.3 fusion
  (8 shorter events, 0.0 us)
Async XLA Ops:
  0.6 7.4 %copy-start = (s32[1,16]{1,0:T(1,128)S(1)}, s32[1,16]{1,0:T(1,128)}, u32[]{:S(2)}) copy-start(s32[1,16]{1,0:T(1,128)} %param.29) | copy-start | bytes 196
  5.8 39.2 %collective-permute-start.17 = (bf16[128,6656]{1,0:T(8,128)(2,1)}, bf16[128,6656]{1,0:T(8,128)(2,1)S(1)}, u32[]{:S(2)}, u32[]{:S(2)}) collective-permute-start(bf16[128,6656]{1,0:T(8,128)(2,1)} %get-tuple-element.67), channel_id=1, source_target_pairs={{0,1},{1,2},{2,3},{3,0},{4,5},{5,6},{6,7},{7,4},{8,9},{9,10},{10,1... | collective-permute-start | bytes 5111816 | tf_op jit(solution)/shard_map/ppermute | solution.py:297
  8.0 39.3 %collective-permute-start.18 = (bf16[128,6656]{1,0:T(8,128)(2,1)}, bf16[128,6656]{1,0:T(8,128)(2,1)}, u32[]{:S(2)}, u32[]{:S(2)}) collective-permute-start(bf16[128,6656]{1,0:T(8,128)(2,1)} %get-tuple-element.68), channel_id=1, source_target_pairs={{0,3},{1,0},{2,1},{3,2},{4,7},{5,4},{6,5},{7,6},{8,11},{9,8},{10,9... | collective-permute-start | bytes 5111816 | tf_op jit(solution)/shard_map/ppermute | solution.py:297
  9.3 17.4 %collective-permute-start.6 = (bf16[14,128,128]{2,1,0:T(8,128)(2,1)S(1)}, bf16[14,128,128]{2,1,0:T(8,128)(2,1)}, u32[]{:S(2)}, u32[]{:S(2)}) collective-permute-start(bf16[14,128,128]{2,1,0:T(8,128)(2,1)S(1)} %param.6), channel_id=1, source_target_pairs={{0,112},{16,96},{32,80},{48,64},{64,48},{80,32},{96,16},{112,0},{1... | collective-permute-start | bytes 1376264 | tf_op jit(solution)/shard_map/cond/branch_6_fun/ppermute | solution.py:324
  30.2 26.0 %collective-permute-start.16 = (bf16[256,1792]{1,0:T(8,128)(2,1)}, bf16[256,1792]{1,0:T(8,128)(2,1)S(1)}, u32[]{:S(2)}, u32[]{:S(2)}) collective-permute-start(bf16[256,1792]{1,0:T(8,128)(2,1)} %new_weights.1.own), channel_id=1, source_target_pairs={{4,8},{8,4},{5,9},{9,5},{6,10},{10,6},{7,11},{11,7},{20,24},{24,20... | collective-permute-start | bytes 2752520 | tf_op jit(solution)/shard_map/ppermute | solution.py:301
  30.9 25.3 %collective-permute-start.15 = (bf16[256,1792]{1,0:T(8,128)(2,1)}, bf16[256,1792]{1,0:T(8,128)(2,1)S(1)}, u32[]{:S(2)}, u32[]{:S(2)}) collective-permute-start(bf16[256,1792]{1,0:T(8,128)(2,1)} %new_weights.1.own), channel_id=1, source_target_pairs={{0,4},{4,0},{8,12},{12,8},{1,5},{5,1},{9,13},{13,9},{2,6},{6,2},{1... | collective-permute-start | bytes 2752520 | tf_op jit(solution)/shard_map/ppermute | solution.py:301
  45.8 17.4 %collective-permute-start.19 = (bf16[128,2816]{1,0:T(8,128)(2,1)}, bf16[128,2816]{1,0:T(8,128)(2,1)}, u32[]{:S(2)}, u32[]{:S(2)}) collective-permute-start(bf16[128,2816]{1,0:T(8,128)(2,1)} %slice.16), channel_id=1, source_target_pairs={{0,1},{1,2},{2,3},{3,0},{4,5},{5,6},{6,7},{7,4},{8,9},{9,10},{10,1... | collective-permute-start | bytes 2162696 | tf_op jit(solution)/shard_map/ppermute | solution.py:297
  49.4 4.0 %copy-start.5 = (bf16[2,128,1024]{2,1,0:T(8,128)(2,1)S(1)}, bf16[2,128,1024]{2,1,0:T(8,128)(2,1)}, u32[]{:S(2)}) copy-start(bf16[2,128,1024]{2,1,0:T(8,128)(2,1)} %get-tuple-element.66) | copy-start | bytes 1572868
  49.4 17.1 %collective-permute-start.20 = (bf16[128,2816]{1,0:T(8,128)(2,1)}, bf16[128,2816]{1,0:T(8,128)(2,1)}, u32[]{:S(2)}, u32[]{:S(2)}) collective-permute-start(bf16[128,2816]{1,0:T(8,128)(2,1)} %slice.17), channel_id=1, source_target_pairs={{0,3},{1,0},{2,1},{3,2},{4,7},{5,4},{6,5},{7,6},{8,11},{9,8},{10,9... | collective-permute-start | bytes 2162696 | tf_op jit(solution)/shard_map/ppermute | solution.py:297
  53.3 1.2 copy-start.4
  56.3 21.7 %collective-permute-start.26 = (bf16[256,1792]{1,0:T(8,128)(2,1)S(1)}, bf16[256,1792]{1,0:T(8,128)(2,1)S(1)}, u32[]{:S(2)}, u32[]{:S(2)}) collective-permute-start(bf16[256,1792]{1,0:T(8,128)(2,1)S(1)} %collective-permute-done.15.beside), channel_id=1, source_target_pairs={{4,8},{8,4},{5,9},{9,5},{6,10},{10,6},{7,11},{11,7},{20,24},{24,20... | collective-permute-start | bytes 2752520 | tf_op jit(solution)/shard_map/ppermute | solution.py:301
  57.0 25.0 %collective-permute-start.27 = (bf16[256,1792]{1,0:T(8,128)(2,1)S(1)}, bf16[256,1792]{1,0:T(8,128)(2,1)S(1)}, u32[]{:S(2)}, u32[]{:S(2)}) collective-permute-start(bf16[256,1792]{1,0:T(8,128)(2,1)S(1)} %collective-permute-done.16.last_inner), channel_id=1, source_target_pairs={{4,0},{8,12},{5,1},{9,13},{6,2},{10,14},{7,3},{11,15},{20,16},{24,... | collective-permute-start | bytes 2752520 | tf_op jit(solution)/shard_map/ppermute | solution.py:301
  72.6 31.3 %copy-start.1 = (bf16[256,1792]{1,0:T(8,128)(2,1)S(1)}, bf16[256,1792]{1,0:T(8,128)(2,1)}, u32[]{:S(2)}) copy-start(bf16[256,1792]{1,0:T(8,128)(2,1)} %new_weights.1.own) | copy-start | bytes 2752516
  72.7 31.3 %copy-start.6 = (s32[2]{0:T(128)S(1)}, s32[2]{0:T(128)}, u32[]{:S(2)}) copy-start(s32[2]{0:T(128)} %pad_add_fusion.where_ref) | copy-start | bytes 28
  72.7 22.8 %collective-permute-start.21 = (bf16[256,1792]{1,0:T(8,128)(2,1)S(1)}, bf16[256,1792]{1,0:T(8,128)(2,1)S(1)}, u32[]{:S(2)}, u32[]{:S(2)}) collective-permute-start(bf16[256,1792]{1,0:T(8,128)(2,1)S(1)} %get-tuple-element.76), channel_id=1, source_target_pairs={{0,4},{12,8},{1,5},{13,9},{2,6},{14,10},{3,7},{15,11},{16,20},{28,... | collective-permute-start | bytes 2752520 | tf_op jit(solution)/shard_map/ppermute | solution.py:301
  82.0 24.3 %collective-permute-start.28 = (bf16[256,1792]{1,0:T(8,128)(2,1)S(1)}, bf16[256,1792]{1,0:T(8,128)(2,1)S(1)}, u32[]{:S(2)}, u32[]{:S(2)}) collective-permute-start(bf16[256,1792]{1,0:T(8,128)(2,1)S(1)} %collective-permute-done.26.mid_inner), channel_id=1, source_target_pairs={{4,0},{8,12},{5,1},{9,13},{6,2},{10,14},{7,3},{11,15},{20,16},{24,... | collective-permute-start | bytes 2752520 | tf_op jit(solution)/shard_map/ppermute | solution.py:301
  95.7 23.0 %collective-permute-start.22 = (bf16[256,1792]{1,0:T(8,128)(2,1)S(1)}, bf16[256,1792]{1,0:T(8,128)(2,1)S(1)}, u32[]{:S(2)}, u32[]{:S(2)}) collective-permute-start(bf16[256,1792]{1,0:T(8,128)(2,1)S(1)} %add_convert_fusion.3), channel_id=1, source_target_pairs={{4,8},{8,4},{5,9},{9,5},{6,10},{10,6},{7,11},{11,7},{20,24},{24,20... | collective-permute-start | bytes 2752520 | tf_op jit(solution)/shard_map/ppermute | solution.py:301
  96.4 27.5 %collective-permute-start.24 = (bf16[256,1792]{1,0:T(8,128)(2,1)S(1)}, bf16[256,1792]{1,0:T(8,128)(2,1)S(1)}, u32[]{:S(2)}, u32[]{:S(2)}) collective-permute-start(bf16[256,1792]{1,0:T(8,128)(2,1)S(1)} %get-tuple-element.78), channel_id=1, source_target_pairs={{0,4},{12,8},{1,5},{13,9},{2,6},{14,10},{3,7},{15,11},{16,20},{28,... | collective-permute-start | bytes 2752520 | tf_op jit(solution)/shard_map/ppermute | solution.py:301
  107.6 25.8 %collective-permute-start.29 = (bf16[256,1792]{1,0:T(8,128)(2,1)S(1)}, bf16[256,1792]{1,0:T(8,128)(2,1)S(1)}, u32[]{:S(2)}, u32[]{:S(2)}) collective-permute-start(bf16[256,1792]{1,0:T(8,128)(2,1)S(1)} %get-tuple-element.88), channel_id=1, source_target_pairs={{0,1},{1,2},{2,3},{3,0},{4,5},{5,6},{6,7},{7,4},{8,9},{9,10},{10,1... | collective-permute-start | bytes 2752520 | tf_op jit(solution)/shard_map/ppermute | solution.py:297
  107.8 25.8 %collective-permute-start.31 = (bf16[256,1792]{1,0:T(8,128)(2,1)S(1)}, bf16[256,1792]{1,0:T(8,128)(2,1)S(1)}, u32[]{:S(2)}, u32[]{:S(2)}) collective-permute-start(bf16[256,1792]{1,0:T(8,128)(2,1)S(1)} %get-tuple-element.89), channel_id=1, source_target_pairs={{0,3},{1,0},{2,1},{3,2},{4,7},{5,4},{6,5},{7,6},{8,11},{9,8},{10,9... | collective-permute-start | bytes 2752520 | tf_op jit(solution)/shard_map/ppermute | solution.py:297
  118.9 26.7 %collective-permute-start.23 = (bf16[256,1792]{1,0:T(8,128)(2,1)S(1)}, bf16[256,1792]{1,0:T(8,128)(2,1)S(1)}, u32[]{:S(2)}, u32[]{:S(2)}) collective-permute-start(bf16[256,1792]{1,0:T(8,128)(2,1)S(1)} %add_convert_fusion.2), channel_id=1, source_target_pairs={{0,4},{4,0},{8,12},{12,8},{1,5},{5,1},{9,13},{13,9},{2,6},{6,2},{1... | collective-permute-start | bytes 2752520 | tf_op jit(solution)/shard_map/ppermute | solution.py:301
  124.1 19.4 %copy-start.2 = (bf16[1,256,1792]{2,1,0:T(8,128)(2,1)S(1)}, bf16[1,256,1792]{2,1,0:T(8,128)(2,1)}, u32[]{:S(2)}) copy-start(bf16[1,256,1792]{2,1,0:T(8,128)(2,1)} %param.26) | copy-start | bytes 2752516
  124.1 19.4 %copy-start.3 = (bf16[1,256,1792]{2,1,0:T(8,128)(2,1)S(1)}, bf16[1,256,1792]{2,1,0:T(8,128)(2,1)}, u32[]{:S(2)}) copy-start(bf16[1,256,1792]{2,1,0:T(8,128)(2,1)} %param.27) | copy-start | bytes 2752516
  124.1 21.5 %collective-permute-start.25 = (bf16[256,1792]{1,0:T(8,128)(2,1)S(1)}, bf16[256,1792]{1,0:T(8,128)(2,1)S(1)}, u32[]{:S(2)}, u32[]{:S(2)}) collective-permute-start(bf16[256,1792]{1,0:T(8,128)(2,1)S(1)} %add_convert_fusion.1), channel_id=1, source_target_pairs={{4,8},{8,4},{5,9},{9,5},{6,10},{10,6},{7,11},{11,7},{20,24},{24,20... | collective-permute-start | bytes 2752520 | tf_op jit(solution)/shard_map/ppermute | solution.py:301
  133.5 9.0 %collective-permute-start.30 = (bf16[128,1792]{1,0:T(8,128)(2,1)S(1)}, bf16[128,1792]{1,0:T(8,128)(2,1)S(1)}, u32[]{:S(2)}, u32[]{:S(2)}) collective-permute-start(bf16[128,1792]{1,0:T(8,128)(2,1)S(1)} %add_convert_fusion.5), channel_id=1, source_target_pairs={{0,1},{1,2},{2,3},{3,0},{4,5},{5,6},{6,7},{7,4},{8,9},{9,10},{10,1... | collective-permute-start | bytes 1376264 | tf_op jit(solution)/shard_map/ppermute | solution.py:297
  133.7 9.8 %collective-permute-start.32 = (bf16[128,1792]{1,0:T(8,128)(2,1)S(1)}, bf16[128,1792]{1,0:T(8,128)(2,1)S(1)}, u32[]{:S(2)}, u32[]{:S(2)}) collective-permute-start(bf16[128,1792]{1,0:T(8,128)(2,1)S(1)} %add_convert_fusion.4), channel_id=1, source_target_pairs={{0,3},{1,0},{2,1},{3,2},{4,7},{5,4},{6,5},{7,6},{8,11},{9,8},{10,9... | collective-permute-start | bytes 1376264 | tf_op jit(solution)/shard_map/ppermute | solution.py:297
